TPU v7x, 256 devices: a whole 4x4x8 slice. The times are simulated.
256 devices in a mesh: replica: 4 (over z_lo, core), fsdp: 64 (over y, z_hi, x).
Axes of the slice: x: 4, y: 4, z: 8 (z_hi: 4, z_lo: 2; z = z_hi * 2 + z_lo), core: 2. Of those that a mesh axis runs over, the one named last changes fastest.
Arguments:
- local_params: bfloat16 [4, 2048, 8192], P('replica', 'fsdp'), may hold values from -6 to 6
- anchor: bfloat16 [2048, 8192], P('fsdp'), may hold values from -6 to 6
- feedback: float32 [4, 2048, 8192], P('replica', 'fsdp'), may hold values from -4 to 4
- master: float32 [2048, 8192], P('fsdp', 'replica'), may hold values from -6 to 6
- momentum: float32 [2048, 8192], P('fsdp', 'replica'), may hold values from -6 to 6
- tokens: bfloat16 [4, 20480, 8192], P('replica', 'fsdp'), may hold values from -16 to 16
- key_weight: bfloat16 [4, 8192, 512], P('replica', 'fsdp'), may hold values from -0.0625 to 0.0625
- key_cotangent: bfloat16 [4, 20480, 512], P('replica', 'fsdp'), may hold values from -0.0390625 to 0.0390625
Outputs:
- master_new: float32 [2048, 8192], P('fsdp', 'replica')
- momentum_new: float32 [2048, 8192], P('fsdp', 'replica')
- anchor_new: bfloat16 [2048, 8192], P('fsdp')
- keys: bfloat16 [4, 20480, 512], P('replica', 'fsdp')
- key_grad: float32 [4, 8192, 512], P('replica', 'fsdp')
All inputs are finite; a program needn't handle non-finite values.
Results may differ from a plain program's by a relative error of at most 0.013.
Values may be sent and summed in bfloat16 or wider, within the bound.
A program may use at most 128 MiB of HBM per device.

v0:
```python
import jax
import jax.numpy as jnp
from jax import lax
from jax.sharding import PartitionSpec as P

LR = 0.7
MU = 0.9


def outer_step(local_params, anchor, feedback, master, momentum):
    corrected = anchor.astype(jnp.float32) - local_params[0].astype(jnp.float32) + feedback[0]
    packed = lax.optimization_barrier(corrected.astype(jnp.bfloat16))
    total = lax.psum_scatter(
        packed.astype(jnp.float32).astype(jnp.bfloat16), "replica", scatter_dimension=1, tiled=True
    ).astype(jnp.float32)
    outer_grad = total / lax.axis_size("replica")
    momentum_new = MU * momentum + outer_grad
    master_new = master - LR * (outer_grad + MU * momentum_new)
    anchor_new = lax.all_gather(master_new.astype(jnp.bfloat16), "replica", axis=1, tiled=True)
    return (master_new, momentum_new, anchor_new)


def inner_step(tokens, key_weight, key_cotangent):
    rows = tokens[0]
    upstream = key_cotangent[0]
    weights = lax.all_gather(key_weight[0], "fsdp", axis=0, tiled=True)
    keys = jnp.dot(rows, weights, preferred_element_type=jnp.float32).astype(jnp.bfloat16)
    term = lax.dot_general(
        rows, upstream, (((0,), (0,)), ((), ())), preferred_element_type=jnp.float32
    )
    key_grad = lax.psum_scatter(term, "fsdp", scatter_dimension=0, tiled=True)
    return (keys[None], key_grad[None])


def on_device(local_params, anchor, feedback, master, momentum, tokens, key_weight, key_cotangent):
    master_new, momentum_new, anchor_new = outer_step(
        local_params, anchor, feedback, master, momentum
    )
    keys, key_grad = inner_step(tokens, key_weight, key_cotangent)
    return (master_new, momentum_new, anchor_new, keys, key_grad)


def solution(mesh):
    in_specs = (
        P("replica", "fsdp", None),
        P("fsdp", None),
        P("replica", "fsdp", None),
        P("fsdp", "replica"),
        P("fsdp", "replica"),
        P("replica", "fsdp", None),
        P("replica", "fsdp", None),
        P("replica", "fsdp", None),
    )
    out_specs = (
        P("fsdp", "replica"),
        P("fsdp", "replica"),
        P("fsdp", None),
        P("replica", "fsdp", None),
        P("replica", "fsdp", None),
    )
    return jax.shard_map(
        on_device, mesh=mesh, in_specs=in_specs, out_specs=out_specs, check_vma=False
    )
```

profile of v0, /device:TPU:32, one launch (start us, length us, event | category | flops | bytes accessed | tf_op | source)
XLA Modules:
  0.0 539.1 jit_solution(11049261495372496917)
XLA Ops:
  8.0 0.0 copy-start
  8.0 0.0 reduce-scatter.3.cloned.1.call-start
  8.1 2.5 fusion.16
  10.6 0.0 reduce-scatter.3.cloned.1.call-update
  10.6 0.0 all-gather.3.cloned.1.call-start
  10.6 0.5 all-gather.3.cloned.1.call-update
  11.2 0.0 reduce-scatter.5.cloned.1.call-start
  11.2 0.0 copy-done
  11.2 10.8 %fusion.2 = f32[8192,512]{1,0:T(8,128)} fusion(bf16[1,320,8192]{2,1,0:T(8,128)(2,1)} %param.13, bf16[1,320,512]{2,1,0:T(8,128)(2,1)S(1)} %copy-done), kind=kOutput, calls=%fused_computation.2 | convolution fusion | flops 2684354560 | bytes 22347776 | tf_op jit(solution)/shard_map/dot_general | solution.py:28
  22.0 0.0 copy-start.1
  22.0 0.0 copy-start.2
  22.0 0.0 reduce-scatter.5.cloned.1.call-update
  22.1 12.2 %reduce-scatter.3.cloned.1.call-done = bf16[32,2048]{1,0:T(8,128)(2,1)} async-done(((bf16[32,8192]{1,0:T(8,128)(2,1)}), bf16[32,2048]{1,0:T(8,128)(2,1)}) %reduce-scatter.3.cloned.1.call-update) | async-done | bytes 131088 | tf_op jit(solution)/shard_map/reduce_scatter | solution.py:13
  34.2 0.0 copy-done.1
  34.2 0.0 copy-done.2
  34.2 1.8 fusion.18
  36.0 8.4 %all_gather.6 = bf16[32,8192]{1,0:T(8,128)(2,1)S(1)} all-gather(bf16[32,2048]{1,0:T(8,128)(2,1)S(1)} %get-tuple-element.5), channel_id=1, replica_groups=mesh['replica'=4,'fsdp'=64] {'replica'}, dimensions={1}, use_global_device_ids=true | all-gather | bytes 655360 | tf_op jit(solution)/shard_map/all_gather | solution.py:19
  44.4 114.8 %all-gather.3.cloned.1.call-done = bf16[1,8192,512]{2,1,0:T(8,128)(2,1)} async-done(((bf16[1,128,512]{2,1,0:T(8,128)(2,1)}), bf16[1,8192,512]{2,1,0:T(8,128)(2,1)}) %all-gather.3.cloned.1.call-update) | async-done | bytes 8388624 | tf_op jit(solution)/shard_map/all_gather | solution.py:26
  159.2 8.6 %fusion.10 = bf16[1,320,512]{2,1,0:T(8,128)(2,1)} fusion(bf16[1,8192,512]{2,1,0:T(8,128)(2,1)} %all-gather.3.cloned.1.call-done, bf16[1,320,8192]{2,1,0:T(8,128)(2,1)} %param.13), kind=kOutput, calls=%fused_computation.6 | convolution fusion | flops 2684518400 | bytes 13959168 | tf_op jit(solution)/shard_map/dot_general | solution.py:27
  167.8 363.0 %reduce-scatter.5.cloned.1.call-done = f32[128,512]{1,0:T(8,128)} async-done(((f32[8192,512]{1,0:T(8,128)}), f32[128,512]{1,0:T(8,128)}) %reduce-scatter.5.cloned.1.call-update) | async-done | bytes 262160 | tf_op jit(solution)/shard_map/reduce_scatter | solution.py:31
  530.8 0.8 copy.14
Async XLA Ops:
  8.0 3.2 copy-start
  8.0 26.2 %reduce-scatter.3.cloned.1.call-start = ((), (), s32[]{:S(2)}) async-start(), calls=%async_computation.2 | async-start | bytes 655360 | tf_op jit(solution)/shard_map/reduce_scatter | solution.py:13
  10.6 148.6 %all-gather.3.cloned.1.call-start = ((), (), s32[]{:S(2)}) async-start(), calls=%async_computation.4 | async-start | bytes 8519680 | tf_op jit(solution)/shard_map/all_gather | solution.py:26
  11.2 519.7 %reduce-scatter.5.cloned.1.call-start = ((), (), s32[]{:S(2)}) async-start(), calls=%async_computation.3 | async-start | bytes 17039360 | tf_op jit(solution)/shard_map/reduce_scatter | solution.py:31
  22.0 12.2 %copy-start.1 = (f32[32,2048]{1,0:T(8,128)S(1)}, f32[32,2048]{1,0:T(8,128)}, u32[]{:S(2)}) copy-start(f32[32,2048]{1,0:T(8,128)} %param.11) | copy-start | bytes 786436
  22.0 12.2 %copy-start.2 = (f32[32,2048]{1,0:T(8,128)S(1)}, f32[32,2048]{1,0:T(8,128)}, u32[]{:S(2)}) copy-start(f32[32,2048]{1,0:T(8,128)} %param.12) | copy-start | bytes 786436
Sparse Core Ops, SparseCore 0:
  12.0 22.2 reduce-scatter.2
  37.3 493.4 reduce-scatter.4
Sparse Core Ops, SparseCore 1:
  14.4 144.8 all-gather.2
where the time goes:
time: 539 us
  waiting for transfers between devices  491 us (91%)
  matrix products  19.4 us (4%)
  between operations  15.5 us (3%)
  blocking collectives  8.42 us (2%)
    reduce_scatter x1, waiting for transfers between devices, inner_step(): key_grad = lax.psum_scatter(term, 'fsdp', scatter_dimension=0, tiled=True)  363 us
    all_gather x1, waiting for transfers between devices, inner_step(): weights = lax.all_gather(key_weight[0], 'fsdp', axis=0, tiled=True)  115 us
    reduce_scatter x1, waiting for transfers between devices, outer_step(): lax.psum_scatter(packed.astype(jnp.float32).astype(jnp.bfloat16), 'replic...  12.2 us
    dot_general x1, matrix products, inner_step(): lax.dot_general(rows, upstream, (((0,), (0,)), ((), ())), preferred_eleme...  10.8 us
  transfers between devices with their start and end apart: 3, of which 3 were waited for; matrix products, arithmetic and copies ran while one was open for 4% of the time, Pallas kernels for 0%

commit v1 on v0

v1 whole, which is shorter than its diff:
```python
import functools

import jax
import jax.numpy as jnp
from jax import lax
from jax.experimental import pallas as pl
from jax.experimental.pallas import tpu as pltpu
from jax.sharding import PartitionSpec as P

LR = 0.7
MU = 0.9
MESH = pl.DeviceIdType.MESH
F32 = jnp.float32
BF16 = jnp.bfloat16
SIDE = 4
BLK = 128
MESSAGES = 150


def kernel(
    lp, an, fb, ms, mo, tk, kw, kc,
    ms_o, mo_o, an_o, keys_o, kg_o,
    W, T, RF, RN, RC, RF2, RN2, RC2, RF3, RN3, RC3,
    tok, cot, cotT, lpv, anv, fbv, msv, mov, pk, RP, AN, msn, mon, acc, keyv, kgv,
    ssem, rsem, lsem,
):
    r = lax.axis_index("replica")
    f = lax.axis_index("fsdp")
    y, z, x = f // 16, (f // 4) % 4, f % 4
    here = {"y": y, "z": z, "x": x}

    def turn(v, s):
        return lax.rem(v + (s % SIDE), SIDE)

    def device(axis, s):
        c = dict(here)
        c[axis] = turn(c[axis], s)
        return (r, (c["y"] * SIDE + c["z"]) * SIDE + c["x"])

    def peer(k):
        return (lax.rem(r + k, 4), f)

    local = []

    def bring(src, dst):
        copy = pltpu.make_async_copy(src, dst, lsem.at[len(local)])
        copy.start()
        local.append(copy)
        return copy

    got_w = [
        bring(kw.at[0, :, pl.ds((2 * d + h) * BLK, BLK)], W.at[y, x, h, d, z])
        for h in range(2) for d in range(2)
    ]
    got_cot = bring(kc.at[0], cot)
    wide = tok.shape[1] // SIDE
    got_tok = {}
    for s in (2, 1, 3, 0):
        cols = pl.ds(pl.multiple_of(turn(y, s) * wide, wide), wide)
        got_tok[s] = bring(tk.at[0, :, cols], tok.at[:, cols])
    got_outer = [bring(an, anv), bring(lp.at[0], lpv), bring(fb.at[0], fbv)]
    got_state = [bring(ms, msv), bring(mo, mov)]

    barrier = pltpu.get_barrier_semaphore()
    partners = [device(axis, s) for axis in "xyz" for s in (1, -1)] + [peer(k) for k in (1, 2, 3)]
    for partner in partners:
        pl.semaphore_signal(barrier, inc=1, device_id=partner, device_id_type=MESH)
    pl.semaphore_wait(barrier, len(partners))

    messages = []

    def send(src, dst, to):
        i = len(messages)
        m = pltpu.make_async_remote_copy(
            src_ref=src, dst_ref=dst, send_sem=ssem.at[i], recv_sem=rsem.at[i],
            device_id=to, device_id_type=MESH,
        )
        m.start()
        messages.append(m)
        return m

    A = ("y", "x")
    B = ("x", "y")
    sent = {}

    def spot(h, a, b):
        return (a, b) if h == 0 else (b, a)

    def z1():
        for c in got_w:
            c.wait()
        for s in (1, -1):
            src = W.at[y, x, :, :, z]
            sent["z1", s] = send(src, src, device("z", s))

    def z2():
        for s in (1, -1):
            sent["z1", s].wait_recv()
            src = W.at[y, x, :, 0 if s == 1 else 1, turn(z, -s)]
            sent["z2", s] = send(src, src, device("z", s))

    def z_end():
        for s in (1, -1):
            sent["z2", s].wait_recv()

    def a1(p):
        for h in range(2):
            for s in (1, -1):
                src = W.at[y, x, h, :, turn(z, p)]
                sent["a1", h, p, s] = send(src, src, device(A[h], s))

    def a2(p):
        for h in range(2):
            for s in (1, -1):
                sent["a1", h, p, s].wait_recv()
                yy, xx = spot(h, turn(here[A[h]], -s), here[B[h]])
                src = W.at[yy, xx, h, 0 if s == 1 else 1, turn(z, p)]
                sent["a2", h, p, s] = send(src, src, device(A[h], s))

    def a_end():
        for h in range(2):
            for p in range(4):
                for s in (1, -1):
                    sent["a2", h, p, s].wait_recv()

    def b1(k):
        for h in range(2):
            for s in (1, -1):
                yy, xx = spot(h, turn(here[A[h]], k), here[B[h]])
                src = W.at[yy, xx, h]
                sent["b1", h, k, s] = send(src, src, device(B[h], s))

    def b2(k):
        for h in range(2):
            for s in (1, -1):
                sent["b1", h, k, s].wait_recv()
                yy, xx = spot(h, turn(here[A[h]], k), turn(here[B[h]], -s))
                src = W.at[yy, xx, h, 0 if s == 1 else 1]
                sent["b2", h, k, s] = send(src, src, device(B[h], s))

    def b_end(k):
        for h in range(2):
            for s in (1, -1):
                sent["b2", h, k, s].wait_recv()

    def tokens_at(yy, zz, xx):
        col = pl.multiple_of(((yy * SIDE + zz) * SIDE + xx) * BLK, BLK)
        return tok[:, pl.ds(col, BLK)]

    def keys(k, j, first=False):
        for h in range(2):
            yy, xx = spot(h, turn(here[A[h]], k), turn(here[B[h]], j))
            left = jnp.concatenate([tokens_at(yy, zz, xx) for zz in range(SIDE)], axis=1)
            right = jnp.concatenate(
                [W[yy, xx, h, d].reshape(SIDE * BLK, BLK) for d in range(2)], axis=1
            )
            part = jnp.dot(left, right, preferred_element_type=F32)
            acc[h] = part if first else acc[h] + part

    def unit(dx, dy):
        if dy in got_tok:
            got_tok.pop(dy).wait()
        yy, xx = turn(y, dy), turn(x, dx)

        @pl.loop(0, 2)
        def _(pair):
            right = jnp.concatenate([tokens_at(yy, 2 * pair + i, xx) for i in range(2)], axis=1)
            res = jnp.dot(cotT[...], right, preferred_element_type=F32).astype(BF16)
            for d in range(2):
                for h in range(2):
                    q = 2 * d + h
                    for i in range(2):
                        T[yy, xx, h, d, 2 * pair + i] = res[
                            q * BLK:(q + 1) * BLK, i * BLK:(i + 1) * BLK
                        ]

    def add4(yy, xx, h, d, others):
        @pl.loop(0, SIDE)
        def _(zz):
            total = T[yy, xx, h, d, zz].astype(F32)
            for ref, lead in others:
                total = total + ref[(*lead, zz)].astype(F32)
            T[yy, xx, h, d, zz] = total.astype(BF16)

    def w(s):
        return 0 if s == 1 else 1

    def far1(h, k):
        a, b = turn(here[A[h]], k), here[B[h]]
        for s in (1, -1):
            yy, xx = spot(h, a, turn(b, 2))
            sent["f1", h, k, s] = send(T.at[yy, xx, h, w(s)], RF.at[h, w(s), a], device(B[h], s))

    def near1(h, k):
        a, b = turn(here[A[h]], k), here[B[h]]
        for s in (1, -1):
            yy, xx = spot(h, a, turn(b, s))
            sent["n1", h, k, s] = send(
                T.at[yy, xx, h, 1 - w(s)], RN.at[h, w(s), a], device(B[h], s)
            )

    def mid1(k):
        for h in range(2):
            a, b = turn(here[A[h]], k), here[B[h]]
            for s in (1, -1):
                yy, xx = spot(h, a, turn(b, s))
                sent["f1", h, k, s].wait_recv()
                add4(yy, xx, h, w(s), [(RF, (h, w(s), a))])
                sent["c1", h, k, s] = send(
                    T.at[yy, xx, h, w(s)], RC.at[h, w(s), a], device(B[h], s)
                )

    def end1(k):
        for h in range(2):
            a, b = turn(here[A[h]], k), here[B[h]]
            yy, xx = spot(h, a, b)
            for s in (1, -1):
                sent["n1", h, k, s].wait_recv()
                sent["c1", h, k, s].wait_recv()
            for s in (1, -1):
                add4(yy, xx, h, w(s), [(RC, (h, w(s), a)), (RN, (h, 1 - w(s), a))])

    def far2():
        for h in range(2):
            yy, xx = spot(h, turn(here[A[h]], 2), here[B[h]])
            for s in (1, -1):
                sent["f2", h, s] = send(T.at[yy, xx, h, w(s)], RF2.at[h, w(s)], device(A[h], s))

    def near2():
        for h in range(2):
            for s in (1, -1):
                yy, xx = spot(h, turn(here[A[h]], s), here[B[h]])
                sent["n2", h, s] = send(T.at[yy, xx, h, 1 - w(s)], RN2.at[h, w(s)], device(A[h], s))

    def mid2():
        for h in range(2):
            for s in (1, -1):
                yy, xx = spot(h, turn(here[A[h]], s), here[B[h]])
                sent["f2", h, s].wait_recv()
                add4(yy, xx, h, w(s), [(RF2, (h, w(s)))])
                sent["c2", h, s] = send(T.at[yy, xx, h, w(s)], RC2.at[h, w(s)], device(A[h], s))

    def end2():
        for h in range(2):
            for s in (1, -1):
                sent["n2", h, s].wait_recv()
                sent["c2", h, s].wait_recv()
            for s in (1, -1):
                add4(y, x, h, w(s), [(RC2, (h, w(s))), (RN2, (h, 1 - w(s)))])

    def start3():
        for h in range(2):
            for s in (1, -1):
                sent["f3", h, s] = send(
                    T.at[y, x, h, w(s), turn(z, 2)], RF3.at[h, w(s)], device("z", s)
                )
            for s in (1, -1):
                sent["n3", h, s] = send(
                    T.at[y, x, h, 1 - w(s), turn(z, s)], RN3.at[h, w(s)], device("z", s)
                )

    def mid3():
        for h in range(2):
            for s in (1, -1):
                sent["f3", h, s].wait_recv()
                zz = turn(z, s)
                T[y, x, h, w(s), zz] = (
                    T[y, x, h, w(s), zz].astype(F32) + RF3[h, w(s)].astype(F32)
                ).astype(BF16)
                sent["c3", h, s] = send(T.at[y, x, h, w(s), zz], RC3.at[h, w(s)], device("z", s))

    def end3():
        for h in range(2):
            for s in (1, -1):
                sent["n3", h, s].wait_recv()
                sent["c3", h, s].wait_recv()
            for s in (1, -1):
                d = w(s)
                total = (
                    T[y, x, h, d, z].astype(F32)
                    + RC3[h, d].astype(F32)
                    + RN3[h, 1 - d].astype(F32)
                )
                kgv[:, (2 * d + h) * BLK:(2 * d + h + 1) * BLK] = total.T

    own = msv.shape[1]

    def outer_send():
        for c in got_outer:
            c.wait()
        for j in range(4):
            cols = slice(j * own, (j + 1) * own)
            corrected = (anv[:, cols].astype(F32) - lpv[:, cols].astype(F32)) + fbv[:, cols]
            pk[j] = corrected.astype(BF16)
        for k in (1, 2, 3):
            sent["pk", k] = send(pk.at[lax.rem(r + k, 4)], RP.at[k - 1], peer(k))

    def outer_step():
        for c in got_state:
            c.wait()
        total = pk[r].astype(F32)
        for k in (1, 2, 3):
            sent["pk", k].wait_recv()
            total = total + RP[k - 1].astype(F32)
        outer_grad = total / 4
        momentum_new = MU * mov[...] + outer_grad
        master_new = msv[...] - LR * (outer_grad + MU * momentum_new)
        mon[...] = momentum_new
        msn[...] = master_new
        AN[r] = master_new.astype(BF16)
        for k in (1, 2, 3):
            sent["an", k] = send(AN.at[r], AN.at[r], peer(k))
        bring(mon, mo_o)
        bring(msn, ms_o)

    def outer_end():
        for k in (1, 2, 3):
            sent["an", k].wait_recv()
        for j in range(4):
            bring(AN.at[j], an_o.at[:, pl.ds(j * own, own)])

    z1()
    a1(0)
    got_cot.wait()
    cotT[...] = cot[...].T
    unit(2, 2)
    far1(0, 2)
    far1(1, 2)
    unit(2, 1)
    far1(0, 1)
    unit(1, 2)
    far1(1, 1)
    unit(2, 3)
    far1(0, 3)
    z2()
    a1(3)
    a1(1)
    unit(3, 2)
    far1(1, 3)
    unit(2, 0)
    far1(0, 0)
    unit(0, 2)
    far1(1, 0)
    near1(0, 2)
    near1(1, 2)
    z_end()
    a1(2)
    a2(0)
    outer_send()
    unit(1, 1)
    unit(3, 1)
    near1(0, 1)
    unit(1, 3)
    near1(1, 1)
    unit(3, 3)
    near1(0, 3)
    near1(1, 3)
    a2(3)
    a2(1)
    mid1(2)
    unit(1, 0)
    unit(3, 0)
    near1(0, 0)
    unit(0, 1)
    unit(0, 3)
    near1(1, 0)
    unit(0, 0)
    a2(2)
    outer_step()
    b1(0)
    mid1(1)
    mid1(3)
    mid1(0)
    a_end()
    b1(3)
    b1(1)
    end1(2)
    far2()
    end1(1)
    end1(3)
    near2()
    b1(2)
    mid2()
    end1(0)
    b2(0)
    outer_end()
    end2()
    start3()
    keys(0, 0, first=True)
    keys(1, 0)
    keys(3, 0)
    keys(2, 0)
    b2(3)
    mid3()
    keys(0, 1)
    keys(0, -1)
    b2(1)
    keys(3, 1)
    keys(3, -1)
    end3()
    bring(kgv, kg_o.at[0])
    b2(2)
    keys(1, 1)
    keys(1, -1)
    b_end(0)
    keys(0, 2)
    b_end(3)
    keys(3, 2)
    keys(2, 1)
    keys(2, -1)
    b_end(1)
    keys(1, 2)
    b_end(2)
    keys(2, 2)
    for h in range(2):
        for d in range(2):
            q = 2 * d + h
            keyv[:, q * BLK:(q + 1) * BLK] = acc[h, :, d * BLK:(d + 1) * BLK].astype(BF16)
    bring(keyv, keys_o.at[0])
    for m in messages:
        m.wait_send()
    waited = len(got_w) + 1 + 4 + len(got_outer) + len(got_state)
    for c in local[waited:]:
        c.wait()


def on_device(lp, an, fb, ms, mo, tk, kw, kc):
    rows, width = an.shape
    own = ms.shape[1]
    tokens, fw = kc.shape[1], kc.shape[2]
    anywhere = pl.BlockSpec(memory_space=pl.ANY)
    out = [
        jax.ShapeDtypeStruct(ms.shape, F32),
        jax.ShapeDtypeStruct(mo.shape, F32),
        jax.ShapeDtypeStruct(an.shape, BF16),
        jax.ShapeDtypeStruct((1, tokens, fw), BF16),
        jax.ShapeDtypeStruct((1, BLK, fw), F32),
    ]
    blocks = (SIDE, SIDE, 2, 2, SIDE, BLK, BLK)
    v = pltpu.VMEM
    scratch = [
        v(blocks, BF16),
        v(blocks, BF16),
        *[v((2, 2, SIDE, SIDE, BLK, BLK), BF16)] * 3,
        *[v((2, 2, SIDE, BLK, BLK), BF16)] * 3,
        *[v((2, 2, BLK, BLK), BF16)] * 3,
        v((tokens, width), BF16),
        v((tokens, fw), BF16),
        v((fw, tokens), BF16),
        v((rows, width), BF16),
        v((rows, width), BF16),
        v((rows, width), F32),
        v((rows, own), F32),
        v((rows, own), F32),
        v((4, rows, own), BF16),
        v((3, rows, own), BF16),
        v((4, rows, own), BF16),
        v((rows, own), F32),
        v((rows, own), F32),
        v((2, tokens, fw // 2), F32),
        v((tokens, fw), BF16),
        v((BLK, fw), F32),
        pltpu.SemaphoreType.DMA((MESSAGES,)),
        pltpu.SemaphoreType.DMA((MESSAGES,)),
        pltpu.SemaphoreType.DMA((32,)),
    ]
    return tuple(
        pl.pallas_call(
            kernel,
            out_shape=out,
            in_specs=[anywhere] * 8,
            out_specs=[anywhere] * 5,
            scratch_shapes=scratch,
            compiler_params=pltpu.CompilerParams(
                collective_id=0, has_side_effects=True, vmem_limit_bytes=60 * 1024 * 1024
            ),
            cost_estimate=pl.CostEstimate(
                flops=4 * tokens * width * fw, bytes_accessed=12 * 1024 * 1024, transcendentals=0
            ),
        )(lp, an, fb, ms, mo, tk, kw, kc)
    )


def solution(mesh):
    in_specs = (
        P("replica", "fsdp", None),
        P("fsdp", None),
        P("replica", "fsdp", None),
        P("fsdp", "replica"),
        P("fsdp", "replica"),
        P("replica", "fsdp", None),
        P("replica", "fsdp", None),
        P("replica", "fsdp", None),
    )
    out_specs = (
        P("fsdp", "replica"),
        P("fsdp", "replica"),
        P("fsdp", None),
        P("replica", "fsdp", None),
        P("replica", "fsdp", None),
    )
    return jax.shard_map(
        on_device, mesh=mesh, in_specs=in_specs, out_specs=out_specs, check_vma=False
    )
```

time: 539 us -> 114 us (0.21)
  waiting for transfers between devices: 491 us -> 0 us
  Pallas kernels: 0 us -> 105 us
  matrix products: 19.4 us -> 0 us
  between operations: 15.5 us -> 0.64 us
  blocking collectives: 8.42 us -> 0 us
  local copies, waits for them, and re-layouts: 0.81 us -> 8.59 us
    reduce_scatter x2 -> x0, waiting for transfers between devices: 375 us -> none  [the longest x1 363 us: inner_step(): key_grad = lax.psum_scatter(term, 'fsdp', scatter_dimension=0, tiled=True)]
    all_gather x1 -> x0, waiting for transfers between devices: 115 us -> none  [inner_step(): weights = lax.all_gather(key_weight[0], 'fsdp', axis=0, tiled=True)]
    pallas_call x0 -> x1, Pallas kernels: none -> 105 us  [on_device(): pl.pallas_call(kernel, out_shape=out, in_specs=[anywhere] * 8, out_specs=...]
    dot_general x2 -> x0, matrix products: 19.4 us -> none  [the longest x1 10.8 us: inner_step(): lax.dot_general(rows, upstream, (((0,), (0,)), ((), ())), preferred_eleme...]
    all_gather x1 -> x0, blocking collectives: 8.42 us -> none  [outer_step(): lax.all_gather(master_new.astype(jnp.bfloat16), 'replica', axis=1, tiled=...]
    unnamed x7 -> x5, local copies, waits for them, and re-layouts: 0.81 us -> 8.59 us
  transfers between devices with their start and end apart: 3 -> 0, of which waited for: 3 -> 0; matrix products, arithmetic and copies ran while one was open for 4% -> 0% of each run, Pallas kernels for 0% -> 0%
where the time goes in v1:
time: 114 us
  Pallas kernels  105 us (92%)
  local copies, waits for them, and re-layouts  8.59 us (8%)
    pallas_call x1, Pallas kernels, on_device(): pl.pallas_call(kernel, out_shape=out, in_specs=[anywhere] * 8, out_specs=...  105 us
    unnamed x5, local copies, waits for them, and re-layouts  8.59 us

profile of v1, /device:TPU:32, one launch (start us, length us, event | category | flops | bytes accessed | tf_op | source)
XLA Modules:
  0.0 114.2 jit_solution(13247265798979699617)
XLA Ops:
  0.6 104.9 %shard_map.119 = (f32[32,2048]{1,0:T(8,128)}, f32[32,2048]{1,0:T(8,128)}, bf16[32,8192]{1,0:T(8,128)(2,1)}, bf16[1,320,512]{2,1,0:T(8,128)(2,1)}, f32[1,128,512]{2,1,0:T(8,128)}) custom-call(bf16[1,32,8192]{2,1,0:T(8,128)(2,1)} %lp.1, bf16[32,8192]{1,0:T(8,128)(2,1)} %an.1, f32[1,32,8192]{2,1,0:T(8,128)} %fb.1, f32[32,2048]{1,0:T(8,128)} %ms.1, ...), custom_call_target="tpu_custom_call" | custom-call | flops 5368709120 | bytes 12582912 | tf_op jit(solution)/shard_map/pallas_call | solution.py:468
  105.6 1.7 %copy.18 = f32[32,2048]{1,0:T(8,128)} copy(f32[32,2048]{1,0:T(8,128)} %get-tuple-element.10) | data formatting | bytes 524288
  107.3 1.7 %copy.19 = f32[32,2048]{1,0:T(8,128)} copy(f32[32,2048]{1,0:T(8,128)} %get-tuple-element.11) | data formatting | bytes 524288
  108.9 1.9 %copy.20 = bf16[32,8192]{1,0:T(8,128)(2,1)} copy(bf16[32,8192]{1,0:T(8,128)(2,1)} %get-tuple-element.12) | data formatting | bytes 1048576
  110.8 1.7 %copy.21 = bf16[1,320,512]{2,1,0:T(8,128)(2,1)} copy(bf16[1,320,512]{2,1,0:T(8,128)(2,1)} %get-tuple-element.13) | data formatting | bytes 655360
  112.5 1.7 %copy.22 = f32[1,128,512]{2,1,0:T(8,128)} copy(f32[1,128,512]{2,1,0:T(8,128)} %get-tuple-element.14) | data formatting | bytes 524288

commit v2 on v0

v2 whole, which is shorter than its diff:
```python
import functools

import jax
import jax.numpy as jnp
from jax import lax
from jax.experimental import pallas as pl
from jax.experimental.pallas import tpu as pltpu
from jax.sharding import PartitionSpec as P

LR = 0.7
MU = 0.9
MESH = pl.DeviceIdType.MESH
F32 = jnp.float32
BF16 = jnp.bfloat16
SIDE = 4
BLK = 128
HALF = BLK // 2
MESSAGES = 144


def kernel(
    lp, an, fb, ms, mo, tk, kw, kc,
    ms_o, mo_o, an_o, keys_o, kg_o,
    X, SP, C, W, T, RF, RN, RC, RF3, RN3, RC3, KA, KS, KR,
    tok, lpv, anv, fbv, msv, mov, pk, RP, AN, msn, mon, keyv, kgv,
    ssem, rsem, lsem,
):
    r = lax.axis_index("replica")
    f = lax.axis_index("fsdp")
    y, z, x = f // 16, (f // 4) % 4, f % 4
    here = {"y": y, "z": z, "x": x}
    E = ("x", "y")
    O = ("y", "x")
    count = tok.shape[0]

    def turn(v, s):
        return lax.rem(v + (s % SIDE), SIDE)

    def device(axis, s):
        c = dict(here)
        c[axis] = turn(c[axis], s)
        return (r, (c["y"] * SIDE + c["z"]) * SIDE + c["x"])

    def peer(k):
        return (lax.rem(r + k, 4), f)

    def rows_of(e):
        return pl.ds(pl.multiple_of(e * count, count), count)

    def w(s):
        return 0 if s == 1 else 1

    local = []

    def bring(src, dst):
        copy = pltpu.make_async_copy(src, dst, lsem.at[len(local)])
        copy.start()
        local.append(copy)
        return copy

    got_w = [
        bring(kw.at[0, pl.ds(h * HALF + d * HALF // 2, HALF // 2)], W.at[h, z, here[O[h]], d])
        for h in range(2) for d in range(2)
    ]
    got_c = [bring(kc.at[0], C.at[h, rows_of(here[E[h]])]) for h in range(2)]
    got_tok = {}
    for k in (2, 1, 3, 0):
        got_tok[k] = []
        for yy in range(SIDE):
            col = pl.multiple_of((yy * SIDE + turn(z, k)) * SIDE * BLK, SIDE * BLK)
            cols = pl.ds(col, SIDE * BLK)
            got_tok[k].append(bring(tk.at[0, :, cols], tok.at[:, cols]))
    got_outer = [bring(an, anv), bring(lp.at[0], lpv), bring(fb.at[0], fbv)]
    got_state = [bring(ms, msv), bring(mo, mov)]
    waited = len(local)

    barrier = pltpu.get_barrier_semaphore()
    partners = (
        [device(axis, s) for axis in "xy" for s in (1, 2, 3)]
        + [device("z", s) for s in (1, 3)]
        + [peer(k) for k in (1, 2, 3)]
    )
    for partner in partners:
        pl.semaphore_signal(barrier, inc=1, device_id=partner, device_id_type=MESH)
    pl.semaphore_wait(barrier, len(partners))

    messages = []
    sent = {}

    def send(key, src, dst, to):
        i = len(messages)
        m = pltpu.make_async_remote_copy(
            src_ref=src, dst_ref=dst, send_sem=ssem.at[i], recv_sem=rsem.at[i],
            device_id=to, device_id_type=MESH,
        )
        m.start()
        messages.append(m)
        sent[key] = m

    def arrived(*key):
        sent[key].wait_recv()

    def c1():
        for h in range(2):
            for s in (1, -1):
                send(("c1", h, s), kc.at[0], C.at[h, rows_of(here[E[h]])], device(E[h], s))

    def c2():
        for h in range(2):
            for s in (1, -1):
                arrived("c1", h, s)
                first = turn(here[E[h]], -s) * count + w(s) * (count // 2)
                src = C.at[h, pl.ds(pl.multiple_of(first, count // 2), count // 2)]
                send(("c2", h, s), src, src, device(E[h], s))

    def c_end():
        for c in got_c:
            c.wait()
        for h in range(2):
            for s in (1, -1):
                arrived("c2", h, s)

    def w1():
        for c in got_w:
            c.wait()
        for h in range(2):
            src = W.at[h, z, here[O[h]]]
            for s in (1, 3, 2):
                send(("w1", h, s), src, src, device(O[h], s))

    def w2(p):
        for h in range(2):
            if p:
                arrived("w1", h, SIDE - p)
            src = W.at[h, z, turn(here[O[h]], p)]
            for s in (1, -1):
                send(("w2", h, p, s), src, src, device("z", s))

    def w3(p):
        for h in range(2):
            for s in (1, -1):
                arrived("w2", h, p, s)
                src = W.at[h, turn(z, -s), turn(here[O[h]], p), w(s)]
                send(("w3", h, p, s), src, src, device("z", s))

    def w_end():
        for h in range(2):
            for p in range(SIDE):
                for s in (1, -1):
                    arrived("w3", h, p, s)

    def pack(h, s, k):
        zz, e = turn(z, k), here[E[h]]
        ee = turn(e, s)
        for i in range(2):
            cols = []
            for oo in (2 * i, 2 * i + 1):
                yy, xx = (oo, ee) if h == 0 else (ee, oo)
                col = ((yy * SIDE + zz) * SIDE + xx) * BLK
                v = tok[:, pl.ds(pl.multiple_of(col, BLK), BLK)]
                cols.append(v[:, :HALF] if h == 0 else v[:, HALF:])
            both = jnp.concatenate(cols, axis=1)
            if s:
                SP[h, s - 1, k, :, i * BLK:(i + 1) * BLK] = both
            else:
                X[h, zz, rows_of(e), i * BLK:(i + 1) * BLK] = both

    def pack_all(k):
        for c in got_tok.pop(k):
            c.wait()
        for s in (2, 1, 3, 0):
            for h in range(2):
                pack(h, s, k)

    def share(k):
        for s in (2, 1, 3):
            for h in range(2):
                send(
                    ("x", h, s, k), SP.at[h, s - 1, k],
                    X.at[h, turn(z, k), rows_of(here[E[h]])], device(E[h], s),
                )

    def shared(h, k):
        for s in (1, 2, 3):
            arrived("x", h, s, k)

    def term(h, k):
        zz = turn(z, k)
        res = lax.dot_general(
            X[h, zz], C[h], (((0,), (0,)), ((), ())), preferred_element_type=F32
        ).astype(BF16)
        T[h, zz] = res.reshape(SIDE, 2, HALF // 2, res.shape[1])

    def far1(h, k):
        zz, o = turn(z, k), here[O[h]]
        for s in (1, -1):
            send(
                ("f1", h, k, s), T.at[h, zz, turn(o, 2), w(s)], RF.at[h, w(s), k],
                device(O[h], s),
            )

    def near1(h, k):
        zz, o = turn(z, k), here[O[h]]
        for s in (1, -1):
            send(
                ("n1", h, k, s), T.at[h, zz, turn(o, s), 1 - w(s)], RN.at[h, w(s), k],
                device(O[h], s),
            )

    def add(zz, h, o, d, others):
        total = T[h, zz, o, d].astype(F32)
        for part in others:
            total = total + part.astype(F32)
        T[h, zz, o, d] = total.astype(BF16)

    def mid1(h, k):
        zz, o = turn(z, k), here[O[h]]
        for s in (1, -1):
            arrived("f1", h, k, s)
            add(zz, h, turn(o, s), w(s), [RF[h, w(s), k]])
            send(
                ("c1", h, k, s), T.at[h, zz, turn(o, s), w(s)], RC.at[h, w(s), k],
                device(O[h], s),
            )

    def end1(h, k):
        zz, o = turn(z, k), here[O[h]]
        for s in (1, -1):
            arrived("n1", h, k, s)
            arrived("c1", h, k, s)
        for d in range(2):
            add(zz, h, o, d, [RC[h, d, k], RN[h, 1 - d, k]])

    def far3(h):
        for s in (1, -1):
            send(
                ("f3", h, s), T.at[h, turn(z, 2), here[O[h]], w(s)], RF3.at[h, w(s)],
                device("z", s),
            )

    def near3(h, s):
        send(
            ("n3", h, s), T.at[h, turn(z, s), here[O[h]], 1 - w(s)], RN3.at[h, w(s)],
            device("z", s),
        )

    def mid3(h, s):
        arrived("f3", h, s)
        add(turn(z, s), h, here[O[h]], w(s), [RF3[h, w(s)]])
        send(
            ("c3", h, s), T.at[h, turn(z, s), here[O[h]], w(s)], RC3.at[h, w(s)],
            device("z", s),
        )

    def end3(h):
        for s in (1, -1):
            arrived("n3", h, s)
            arrived("c3", h, s)
        for d in range(2):
            first = h * HALF + d * HALF // 2
            kgv[first:first + HALF // 2, :] = (
                T[h, z, here[O[h]], d].astype(F32)
                + RC3[h, d].astype(F32)
                + RN3[h, 1 - d].astype(F32)
            )

    def keys(h, s, ks, first, last):
        e = turn(here[E[h]], s)
        left = jnp.concatenate([X[h, turn(z, k), rows_of(e)] for k in ks], axis=1)
        right = jnp.concatenate(
            [W[h, turn(z, k)].reshape(2 * BLK, W.shape[-1]) for k in ks], axis=0
        )
        total = jnp.dot(left, right, preferred_element_type=F32)
        if not first:
            total = total + KA[h, s]
        if last and s:
            KS[h, s - 1] = total.astype(BF16)
            send(("k", h, s), KS.at[h, s - 1], KR.at[h, s - 1], device(E[h], s))
        else:
            KA[h, s] = total

    def keys_end():
        total = KA[0, 0] + KA[1, 0]
        for h in range(2):
            for s in (1, 3, 2):
                arrived("k", h, s)
                total = total + KR[h, s - 1].astype(F32)
        keyv[...] = total.astype(BF16)
        bring(keyv, keys_o.at[0])

    own = msv.shape[1]

    def outer_send():
        for c in got_outer:
            c.wait()
        for j in range(4):
            cols = slice(j * own, (j + 1) * own)
            corrected = (anv[:, cols].astype(F32) - lpv[:, cols].astype(F32)) + fbv[:, cols]
            pk[j] = corrected.astype(BF16)
        for k in (1, 2, 3):
            send(("pk", k), pk.at[lax.rem(r + k, 4)], RP.at[k - 1], peer(k))

    def outer_step():
        for c in got_state:
            c.wait()
        total = pk[r].astype(F32)
        for k in (1, 2, 3):
            arrived("pk", k)
            total = total + RP[k - 1].astype(F32)
        outer_grad = total / 4
        momentum_new = MU * mov[...] + outer_grad
        master_new = msv[...] - LR * (outer_grad + MU * momentum_new)
        mon[...] = momentum_new
        msn[...] = master_new
        AN[r] = master_new.astype(BF16)
        for k in (1, 2, 3):
            send(("an", k), AN.at[r], AN.at[r], peer(k))
        bring(mon, mo_o)
        bring(msn, ms_o)

    def outer_end():
        for k in (1, 2, 3):
            arrived("an", k)
        for j in range(4):
            bring(AN.at[j], an_o.at[:, pl.ds(j * own, own)])

    def both(step, *args):
        for h in range(2):
            step(h, *args)

    def terms(k):
        for h in range(2):
            term(h, k)
            far1(h, k)
            near1(h, k)

    w1()
    c1()
    pack_all(2)
    share(2)
    w2(0)
    pack_all(1)
    share(1)
    w2(1)
    w2(3)
    w2(2)
    c2()
    pack_all(3)
    share(3)
    w3(0)
    pack_all(0)
    share(0)
    outer_send()
    w3(1)
    c_end()
    both(shared, 2)
    terms(2)
    w3(3)
    both(shared, 1)
    terms(1)
    w3(2)
    outer_step()

    both(shared, 3)
    terms(3)
    w_end()
    for s in (2, 1, 3, 0):
        both(keys, s, (2, 1), True, False)
    both(shared, 0)
    terms(0)
    both(mid1, 2)
    both(mid1, 1)
    for s in (2, 1, 3):
        both(keys, s, (3, 0), False, True)

    both(mid1, 3)
    both(end1, 2)
    both(far3)
    both(end1, 1)
    both(near3, 1)
    both(mid3, 1)
    both(mid1, 0)
    both(end1, 3)
    both(near3, -1)
    both(mid3, -1)
    both(keys, 0, (3, 0), False, False)
    both(end1, 0)
    both(end3)
    bring(kgv, kg_o.at[0])
    outer_end()
    keys_end()
    for m in messages:
        m.wait_send()
    for c in local[waited:]:
        c.wait()


def hand_over(*refs):
    sources, results, held, sems = refs[:5], refs[5:10], refs[10:15], refs[15]
    inward = [pltpu.make_async_copy(a, b, sems.at[0, i]) for i, (a, b) in enumerate(zip(sources, held))]
    outward = [pltpu.make_async_copy(a, b, sems.at[1, i]) for i, (a, b) in enumerate(zip(held, results))]
    for c in inward:
        c.start()
    for c, o in zip(inward, outward):
        c.wait()
        o.start()
    for o in outward:
        o.wait()


def on_device(lp, an, fb, ms, mo, tk, kw, kc):
    rows, width = an.shape
    own = ms.shape[1]
    tokens, fw = kc.shape[1], kc.shape[2]
    anywhere = pl.BlockSpec(memory_space=pl.ANY)
    out = [
        jax.ShapeDtypeStruct(ms.shape, F32),
        jax.ShapeDtypeStruct(mo.shape, F32),
        jax.ShapeDtypeStruct(an.shape, BF16),
        jax.ShapeDtypeStruct((1, tokens, fw), BF16),
        jax.ShapeDtypeStruct((1, BLK, fw), F32),
    ]
    v = pltpu.VMEM
    piece = (HALF // 2, fw)
    scratch = [
        v((2, SIDE, SIDE * tokens, SIDE * HALF), BF16),
        v((2, SIDE - 1, SIDE, tokens, SIDE * HALF), BF16),
        v((2, SIDE * tokens, fw), BF16),
        *[v((2, SIDE, SIDE, 2, *piece), BF16)] * 2,
        *[v((2, 2, SIDE, *piece), BF16)] * 3,
        *[v((2, 2, *piece), BF16)] * 3,
        v((2, SIDE, tokens, fw), F32),
        *[v((2, SIDE - 1, tokens, fw), BF16)] * 2,
        v((tokens, width), BF16),
        v((rows, width), BF16),
        v((rows, width), BF16),
        v((rows, width), F32),
        v((rows, own), F32),
        v((rows, own), F32),
        v((4, rows, own), BF16),
        v((3, rows, own), BF16),
        v((4, rows, own), BF16),
        v((rows, own), F32),
        v((rows, own), F32),
        v((tokens, fw), BF16),
        v((BLK, fw), F32),
        pltpu.SemaphoreType.DMA((MESSAGES,)),
        pltpu.SemaphoreType.DMA((MESSAGES,)),
        pltpu.SemaphoreType.DMA((36,)),
    ]
    done = pl.pallas_call(
        kernel,
        out_shape=out,
        in_specs=[anywhere] * 8,
        out_specs=[anywhere] * 5,
        scratch_shapes=scratch,
        compiler_params=pltpu.CompilerParams(
            collective_id=0, has_side_effects=True, vmem_limit_bytes=60 * 1024 * 1024
        ),
        cost_estimate=pl.CostEstimate(
            flops=4 * tokens * width * fw, bytes_accessed=12 * 1024 * 1024, transcendentals=0
        ),
    )(lp, an, fb, ms, mo, tk, kw, kc)
    return tuple(
        pl.pallas_call(
            hand_over,
            out_shape=out,
            in_specs=[anywhere] * 5,
            out_specs=[anywhere] * 5,
            scratch_shapes=[*[v(o.shape, o.dtype) for o in out], pltpu.SemaphoreType.DMA((2, 5))],
        )(*done)
    )


def solution(mesh):
    in_specs = (
        P("replica", "fsdp", None),
        P("fsdp", None),
        P("replica", "fsdp", None),
        P("fsdp", "replica"),
        P("fsdp", "replica"),
        P("replica", "fsdp", None),
        P("replica", "fsdp", None),
        P("replica", "fsdp", None),
    )
    out_specs = (
        P("fsdp", "replica"),
        P("fsdp", "replica"),
        P("fsdp", None),
        P("replica", "fsdp", None),
        P("replica", "fsdp", None),
    )
    return jax.shard_map(
        on_device, mesh=mesh, in_specs=in_specs, out_specs=out_specs, check_vma=False
    )
```

time: 539 us -> 87.6 us (0.16)
  waiting for transfers between devices: 491 us -> 0 us
  Pallas kernels: 0 us -> 85.2 us
  matrix products: 19.4 us -> 0 us
  between operations: 15.5 us -> 0.64 us
  blocking collectives: 8.42 us -> 0 us
    reduce_scatter x2 -> x0, waiting for transfers between devices: 375 us -> none  [the longest x1 363 us: inner_step(): key_grad = lax.psum_scatter(term, 'fsdp', scatter_dimension=0, tiled=True)]
    all_gather x1 -> x0, waiting for transfers between devices: 115 us -> none  [inner_step(): weights = lax.all_gather(key_weight[0], 'fsdp', axis=0, tiled=True)]
    pallas_call x0 -> x2, Pallas kernels: none -> 85.2 us  [the longest x1 83 us: on_device(): pl.pallas_call(kernel, out_shape=out, in_specs=[anywhere] * 8, out_specs=...]
    dot_general x2 -> x0, matrix products: 19.4 us -> none  [the longest x1 10.8 us: inner_step(): lax.dot_general(rows, upstream, (((0,), (0,)), ((), ())), preferred_eleme...]
    all_gather x1 -> x0, blocking collectives: 8.42 us -> none  [outer_step(): lax.all_gather(master_new.astype(jnp.bfloat16), 'replica', axis=1, tiled=...]
  transfers between devices with their start and end apart: 3 -> 0, of which waited for: 3 -> 0; matrix products, arithmetic and copies ran while one was open for 4% -> 0% of each run, Pallas kernels for 0% -> 0%
where the time goes in v2:
time: 87.6 us; the launch traced here: 85.9 us
  Pallas kernels  85.2 us (97%)
    pallas_call x1, Pallas kernels, on_device(): pl.pallas_call(kernel, out_shape=out, in_specs=[anywhere] * 8, out_specs=...  83 us
    pallas_call x1, Pallas kernels, on_device(): pl.pallas_call(hand_over, out_shape=out, in_specs=[anywhere] * 5, out_spe...  2.27 us

profile of v2, /device:TPU:32, one launch (start us, length us, event | category | flops | bytes accessed | tf_op | source)
XLA Modules:
  0.0 85.9 jit_solution(9996999586984350193)
XLA Ops:
  0.6 83.0 %shard_map.119 = (f32[32,2048]{1,0:T(8,128)}, f32[32,2048]{1,0:T(8,128)}, bf16[32,8192]{1,0:T(8,128)(2,1)}, bf16[1,320,512]{2,1,0:T(8,128)(2,1)}, f32[1,128,512]{2,1,0:T(8,128)}) custom-call(bf16[1,32,8192]{2,1,0:T(8,128)(2,1)} %lp.1, bf16[32,8192]{1,0:T(8,128)(2,1)} %an.1, f32[1,32,8192]{2,1,0:T(8,128)} %fb.1, f32[32,2048]{1,0:T(8,128)} %ms.1, ...), custom_call_target="tpu_custom_call" | custom-call | flops 5368709120 | bytes 12582912 | tf_op jit(solution)/shard_map/pallas_call | solution.py:451
  83.6 2.3 %shard_map.120 = (f32[32,2048]{1,0:T(8,128)}, f32[32,2048]{1,0:T(8,128)}, bf16[32,8192]{1,0:T(8,128)(2,1)}, bf16[1,320,512]{2,1,0:T(8,128)(2,1)}, f32[1,128,512]{2,1,0:T(8,128)}) custom-call(f32[32,2048]{1,0:T(8,128)} %get-tuple-element.10.refs_0_, f32[32,2048]{1,0:T(8,128)} %get-tuple-element.11.refs_1_, bf16[32,8192]{1,0:T(8,128)(2,1)} %get-tuple-element.12.refs_2_, ...), custom_call_target="tpu_custom_call" | custom-call | tf_op jit(solution)/shard_map/pallas_call | solution.py:465

commit v3 on v2

--- a/solution.py
+++ b/solution.py
@@ -15,14 +15,14 @@
 SIDE = 4
 BLK = 128
 HALF = BLK // 2
-MESSAGES = 144
+MESSAGES = 148
 
 
 def kernel(
     lp, an, fb, ms, mo, tk, kw, kc,
     ms_o, mo_o, an_o, keys_o, kg_o,
-    X, SP, C, W, T, RF, RN, RC, RF3, RN3, RC3, KA, KS, KR,
-    tok, lpv, anv, fbv, msv, mov, pk, RP, AN, msn, mon, keyv, kgv,
+    X, SP, C, W, T, RF, RN, RC, RF3, RN3, RC3, KA, KS, KF, KN, KC,
+    tok, lpv, anv, fbv, msv, mov, pk, RP, AN,
     ssem, rsem, lsem,
 ):
     r = lax.axis_index("replica")
@@ -72,7 +72,6 @@
             got_tok[k].append(bring(tk.at[0, :, cols], tok.at[:, cols]))
     got_outer = [bring(an, anv), bring(lp.at[0], lpv), bring(fb.at[0], fbv)]
     got_state = [bring(ms, msv), bring(mo, mov)]
-    waited = len(local)
 
     barrier = pltpu.get_barrier_semaphore()
     partners = (
@@ -258,7 +257,7 @@
             arrived("c3", h, s)
         for d in range(2):
             first = h * HALF + d * HALF // 2
-            kgv[first:first + HALF // 2, :] = (
+            kg_o[0, first:first + HALF // 2, :] = (
                 T[h, z, here[O[h]], d].astype(F32)
                 + RC3[h, d].astype(F32)
                 + RN3[h, 1 - d].astype(F32)
@@ -273,20 +272,45 @@
         total = jnp.dot(left, right, preferred_element_type=F32)
         if not first:
             total = total + KA[h, s]
-        if last and s:
-            KS[h, s - 1] = total.astype(BF16)
-            send(("k", h, s), KS.at[h, s - 1], KR.at[h, s - 1], device(E[h], s))
+        if not last or s == 0:
+            KA[h, s] = total
+            return
+        step = count // 2
+        KS[h, s - 1] = total.astype(BF16)
+        if s == 2:
+            for t in (1, -1):
+                send(
+                    ("kf", h, t), KS.at[h, 1, pl.ds(w(t) * step, step)], KF.at[h, w(t)],
+                    device(E[h], t),
+                )
         else:
+            t = 1 if s == 1 else -1
             KA[h, s] = total
+            send(
+                ("kn", h, t), KS.at[h, s - 1, pl.ds((1 - w(t)) * step, step)], KN.at[h, w(t)],
+                device(E[h], t),
+            )
+
+    def keys_mid(h):
+        step = count // 2
+        for t in (1, -1):
+            s, rows = t % SIDE, pl.ds(w(t) * step, step)
+            arrived("kf", h, t)
+            KS[h, s - 1, rows] = (KA[h, s, rows] + KF[h, w(t)].astype(F32)).astype(BF16)
+            send(("kc", h, t), KS.at[h, s - 1, rows], KC.at[h, w(t)], device(E[h], t))
 
     def keys_end():
-        total = KA[0, 0] + KA[1, 0]
-        for h in range(2):
-            for s in (1, 3, 2):
-                arrived("k", h, s)
-                total = total + KR[h, s - 1].astype(F32)
-        keyv[...] = total.astype(BF16)
-        bring(keyv, keys_o.at[0])
+        step = count // 2
+        for h in range(2):
+            for t in (1, -1):
+                arrived("kn", h, t)
+        for d in range(2):
+            rows = pl.ds(d * step, step)
+            total = KA[0, 0, rows] + KA[1, 0, rows]
+            for h in range(2):
+                arrived("kc", h, 1 - 2 * d)
+                total = total + KN[h, 1 - d].astype(F32) + KC[h, d].astype(F32)
+            keys_o[0, rows] = total.astype(BF16)
 
     own = msv.shape[1]
 
@@ -310,19 +334,17 @@
         outer_grad = total / 4
         momentum_new = MU * mov[...] + outer_grad
         master_new = msv[...] - LR * (outer_grad + MU * momentum_new)
-        mon[...] = momentum_new
-        msn[...] = master_new
+        mo_o[...] = momentum_new
+        ms_o[...] = master_new
         AN[r] = master_new.astype(BF16)
         for k in (1, 2, 3):
             send(("an", k), AN.at[r], AN.at[r], peer(k))
-        bring(mon, mo_o)
-        bring(msn, ms_o)
 
     def outer_end():
         for k in (1, 2, 3):
             arrived("an", k)
         for j in range(4):
-            bring(AN.at[j], an_o.at[:, pl.ds(j * own, own)])
+            an_o[:, j * own:(j + 1) * own] = AN[j]
 
     def both(step, *args):
         for h in range(2):
@@ -376,6 +398,7 @@
     both(mid1, 3)
     both(end1, 2)
     both(far3)
+    both(keys_mid)
     both(end1, 1)
     both(near3, 1)
     both(mid3, 1)
@@ -386,26 +409,19 @@
     both(keys, 0, (3, 0), False, False)
     both(end1, 0)
     both(end3)
-    bring(kgv, kg_o.at[0])
     outer_end()
     keys_end()
     for m in messages:
         m.wait_send()
-    for c in local[waited:]:
+
+
+def hand_over(*refs):
+    sources, results, sems = refs[:5], refs[5:10], refs[10]
+    copies = [pltpu.make_async_copy(a, b, sems.at[i]) for i, (a, b) in enumerate(zip(sources, results))]
+    for c in copies:
+        c.start()
+    for c in copies:
         c.wait()
-
-
-def hand_over(*refs):
-    sources, results, held, sems = refs[:5], refs[5:10], refs[10:15], refs[15]
-    inward = [pltpu.make_async_copy(a, b, sems.at[0, i]) for i, (a, b) in enumerate(zip(sources, held))]
-    outward = [pltpu.make_async_copy(a, b, sems.at[1, i]) for i, (a, b) in enumerate(zip(held, results))]
-    for c in inward:
-        c.start()
-    for c, o in zip(inward, outward):
-        c.wait()
-        o.start()
-    for o in outward:
-        o.wait()
 
 
 def on_device(lp, an, fb, ms, mo, tk, kw, kc):
@@ -430,7 +446,8 @@
         *[v((2, 2, SIDE, *piece), BF16)] * 3,
         *[v((2, 2, *piece), BF16)] * 3,
         v((2, SIDE, tokens, fw), F32),
-        *[v((2, SIDE - 1, tokens, fw), BF16)] * 2,
+        v((2, SIDE - 1, tokens, fw), BF16),
+        *[v((2, 2, tokens // 2, fw), BF16)] * 3,
         v((tokens, width), BF16),
         v((rows, width), BF16),
         v((rows, width), BF16),
@@ -440,19 +457,15 @@
         v((4, rows, own), BF16),
         v((3, rows, own), BF16),
         v((4, rows, own), BF16),
-        v((rows, own), F32),
-        v((rows, own), F32),
-        v((tokens, fw), BF16),
-        v((BLK, fw), F32),
         pltpu.SemaphoreType.DMA((MESSAGES,)),
         pltpu.SemaphoreType.DMA((MESSAGES,)),
-        pltpu.SemaphoreType.DMA((36,)),
+        pltpu.SemaphoreType.DMA((27,)),
     ]
     done = pl.pallas_call(
         kernel,
-        out_shape=out,
+        out_shape=[v(o.shape, o.dtype) for o in out],
         in_specs=[anywhere] * 8,
-        out_specs=[anywhere] * 5,
+        out_specs=[pl.BlockSpec(memory_space=pltpu.VMEM)] * 5,
         scratch_shapes=scratch,
         compiler_params=pltpu.CompilerParams(
             collective_id=0, has_side_effects=True, vmem_limit_bytes=60 * 1024 * 1024
@@ -465,10 +478,10 @@
         pl.pallas_call(
             hand_over,
             out_shape=out,
-            in_specs=[anywhere] * 5,
+            in_specs=[pl.BlockSpec(memory_space=pltpu.VMEM)] * 5,
             out_specs=[anywhere] * 5,
-            scratch_shapes=[*[v(o.shape, o.dtype) for o in out], pltpu.SemaphoreType.DMA((2, 5))],
-        )(*done)
+            scratch_shapes=[pltpu.SemaphoreType.DMA((5,))],
+        )(*[pltpu.with_memory_space_constraint(o, pltpu.VMEM) for o in done])
     )
 
 

time: 87.6 us -> 78.6 us (0.90); the launches traced: 85.9 us -> 78.5 us
  Pallas kernels: 85.2 us -> 77.8 us
    pallas_call x2, Pallas kernels: 85.2 us -> 77.8 us  [the longest x1 76.6 us: on_device(): pl.pallas_call(kernel, out_shape=[v(o.shape, o.dtype) for o in out], in_s...]
where the time goes in v3:
time: 78.6 us; the launch traced here: 78.5 us
  Pallas kernels  77.8 us (99%)
    pallas_call x1, Pallas kernels, on_device(): pl.pallas_call(kernel, out_shape=[v(o.shape, o.dtype) for o in out], in_s...  76.6 us

profile of v3, /device:TPU:32, one launch (start us, length us, event | category | flops | bytes accessed | tf_op | source)
XLA Modules:
  0.0 78.5 jit_solution(10135232325591354833)
XLA Ops:
  0.6 76.6 %shard_map.119 = (f32[32,2048]{1,0:T(8,128)S(1)}, f32[32,2048]{1,0:T(8,128)S(1)}, bf16[32,8192]{1,0:T(8,128)(2,1)S(1)}, bf16[1,320,512]{2,1,0:T(8,128)(2,1)S(1)}, f32[1,128,512]{2,1,0:T(8,128)S(1)}) custom-call(bf16[1,32,8192]{2,1,0:T(8,128)(2,1)} %lp.1, bf16[32,8192]{1,0:T(8,128)(2,1)} %an.1, f32[1,32,8192]{2,1,0:T(8,128)} %fb.1, f32[32,2048]{1,0:T(8,128)} %ms.1, ...), custom_call_target="tpu_custom_call" | custom-call | flops 5368709120 | bytes 12582912 | tf_op jit(solution)/shard_map/pallas_call | solution.py:464
  77.3 1.2 %shard_map.120 = (f32[32,2048]{1,0:T(8,128)}, f32[32,2048]{1,0:T(8,128)}, bf16[32,8192]{1,0:T(8,128)(2,1)}, bf16[1,320,512]{2,1,0:T(8,128)(2,1)}, f32[1,128,512]{2,1,0:T(8,128)}) custom-call(f32[32,2048]{1,0:T(8,128)S(1)} %get-tuple-element.10.refs_0_, f32[32,2048]{1,0:T(8,128)S(1)} %get-tuple-element.11.refs_1_, ...), custom_call_target="tpu_custom_call" | custom-call | tf_op jit(solution)/shard_map/pallas_call | solution.py:478

commit v4 on v3

--- a/solution.py
+++ b/solution.py
@@ -50,6 +50,15 @@
     def w(s):
         return 0 if s == 1 else 1
 
+    barrier = pltpu.get_barrier_semaphore()
+    partners = (
+        [device(axis, s) for axis in "xy" for s in (1, 2, 3)]
+        + [device("z", s) for s in (1, 3)]
+        + [peer(k) for k in (1, 2, 3)]
+    )
+    for partner in partners:
+        pl.semaphore_signal(barrier, inc=1, device_id=partner, device_id_type=MESH)
+
     local = []
 
     def bring(src, dst):
@@ -73,14 +82,6 @@
     got_outer = [bring(an, anv), bring(lp.at[0], lpv), bring(fb.at[0], fbv)]
     got_state = [bring(ms, msv), bring(mo, mov)]
 
-    barrier = pltpu.get_barrier_semaphore()
-    partners = (
-        [device(axis, s) for axis in "xy" for s in (1, 2, 3)]
-        + [device("z", s) for s in (1, 3)]
-        + [peer(k) for k in (1, 2, 3)]
-    )
-    for partner in partners:
-        pl.semaphore_signal(barrier, inc=1, device_id=partner, device_id_type=MESH)
     pl.semaphore_wait(barrier, len(partners))
 
     messages = []
@@ -98,6 +99,13 @@
 
     def arrived(*key):
         sent[key].wait_recv()
+
+    drained = []
+
+    def drain():
+        for m in messages[len(drained):]:
+            m.wait_send()
+            drained.append(m)
 
     def c1():
         for h in range(2):
@@ -263,16 +271,14 @@
                 + RN3[h, 1 - d].astype(F32)
             )
 
-    def keys(h, s, ks, first, last):
+    def keys(h, s):
         e = turn(here[E[h]], s)
-        left = jnp.concatenate([X[h, turn(z, k), rows_of(e)] for k in ks], axis=1)
+        left = jnp.concatenate([X[h, turn(z, k), rows_of(e)] for k in range(SIDE)], axis=1)
         right = jnp.concatenate(
-            [W[h, turn(z, k)].reshape(2 * BLK, W.shape[-1]) for k in ks], axis=0
+            [W[h, turn(z, k)].reshape(2 * BLK, W.shape[-1]) for k in range(SIDE)], axis=0
         )
         total = jnp.dot(left, right, preferred_element_type=F32)
-        if not first:
-            total = total + KA[h, s]
-        if not last or s == 0:
+        if s == 0:
             KA[h, s] = total
             return
         step = count // 2
@@ -358,9 +364,9 @@
 
     w1()
     c1()
+    w2(0)
     pack_all(2)
     share(2)
-    w2(0)
     pack_all(1)
     share(1)
     w2(1)
@@ -381,38 +387,35 @@
     both(shared, 1)
     terms(1)
     w3(2)
-    outer_step()
-
     both(shared, 3)
     terms(3)
-    w_end()
-    for s in (2, 1, 3, 0):
-        both(keys, s, (2, 1), True, False)
     both(shared, 0)
     terms(0)
+    outer_step()
     both(mid1, 2)
     both(mid1, 1)
-    for s in (2, 1, 3):
-        both(keys, s, (3, 0), False, True)
-
+    w_end()
+    both(keys, 2)
     both(mid1, 3)
+    both(mid1, 0)
+    both(keys, 1)
+    both(keys, 3)
     both(end1, 2)
     both(far3)
-    both(keys_mid)
     both(end1, 1)
     both(near3, 1)
-    both(mid3, 1)
-    both(mid1, 0)
     both(end1, 3)
     both(near3, -1)
+    both(keys_mid)
+    both(mid3, 1)
     both(mid3, -1)
-    both(keys, 0, (3, 0), False, False)
+    both(keys, 0)
+    outer_end()
+    drain()
     both(end1, 0)
     both(end3)
-    outer_end()
     keys_end()
-    for m in messages:
-        m.wait_send()
+    drain()
 
 
 def hand_over(*refs):

time: 78.6 us -> 75.3 us (0.958)
  Pallas kernels: 77.8 us -> 73.9 us
    pallas_call x1, Pallas kernels: 76.6 us -> 72.7 us  [on_device(): pl.pallas_call(kernel, out_shape=[v(o.shape, o.dtype) for o in out], in_s...]
where the time goes in v4:
time: 75.3 us; the launch traced here: 74.5 us
  Pallas kernels  73.9 us (98%)
    pallas_call x1, Pallas kernels, on_device(): pl.pallas_call(kernel, out_shape=[v(o.shape, o.dtype) for o in out], in_s...  72.7 us

profile of v4, /device:TPU:32, one launch (start us, length us, event | category | flops | bytes accessed | tf_op | source)
XLA Modules:
  0.0 74.5 jit_solution(3639162508514734442)
XLA Ops:
  0.6 72.7 %shard_map.119 = (f32[32,2048]{1,0:T(8,128)S(1)}, f32[32,2048]{1,0:T(8,128)S(1)}, bf16[32,8192]{1,0:T(8,128)(2,1)S(1)}, bf16[1,320,512]{2,1,0:T(8,128)(2,1)S(1)}, f32[1,128,512]{2,1,0:T(8,128)S(1)}) custom-call(bf16[1,32,8192]{2,1,0:T(8,128)(2,1)} %lp.1, bf16[32,8192]{1,0:T(8,128)(2,1)} %an.1, f32[1,32,8192]{2,1,0:T(8,128)} %fb.1, f32[32,2048]{1,0:T(8,128)} %ms.1, ...), custom_call_target="tpu_custom_call" | custom-call | flops 5368709120 | bytes 12582912 | tf_op jit(solution)/shard_map/pallas_call | solution.py:467
  73.3 1.2 %shard_map.120 = (f32[32,2048]{1,0:T(8,128)}, f32[32,2048]{1,0:T(8,128)}, bf16[32,8192]{1,0:T(8,128)(2,1)}, bf16[1,320,512]{2,1,0:T(8,128)(2,1)}, f32[1,128,512]{2,1,0:T(8,128)}) custom-call(f32[32,2048]{1,0:T(8,128)S(1)} %get-tuple-element.10.refs_0_, f32[32,2048]{1,0:T(8,128)S(1)} %get-tuple-element.11.refs_1_, ...), custom_call_target="tpu_custom_call" | custom-call | tf_op jit(solution)/shard_map/pallas_call | solution.py:481

commit v5 on v4

--- a/solution.py
+++ b/solution.py
@@ -15,7 +15,7 @@
 SIDE = 4
 BLK = 128
 HALF = BLK // 2
-MESSAGES = 148
+MESSAGES = 150
 
 
 def kernel(
@@ -132,13 +132,21 @@
             c.wait()
         for h in range(2):
             src = W.at[h, z, here[O[h]]]
-            for s in (1, 3, 2):
+            for s in (1, -1):
                 send(("w1", h, s), src, src, device(O[h], s))
 
+    def w1_on():
+        for h in range(2):
+            for s in (1, -1):
+                arrived("w1", h, s)
+                src = W.at[h, z, turn(here[O[h]], -s), w(s)]
+                send(("w1", h, s, "on"), src, src, device(O[h], s))
+
     def w2(p):
         for h in range(2):
-            if p:
-                arrived("w1", h, SIDE - p)
+            if p == 2:
+                for s in (1, -1):
+                    arrived("w1", h, s, "on")
             src = W.at[h, z, turn(here[O[h]], p)]
             for s in (1, -1):
                 send(("w2", h, p, s), src, src, device("z", s))
@@ -369,15 +377,16 @@
     share(2)
     pack_all(1)
     share(1)
+    w1_on()
     w2(1)
     w2(3)
-    w2(2)
     c2()
     pack_all(3)
     share(3)
     w3(0)
     pack_all(0)
     share(0)
+    w2(2)
     outer_send()
     w3(1)
     c_end()

time: 75.3 us -> 74.9 us (level)
  no operation moved by 1% of the time
where the time goes in v5:
time: 74.9 us; the launch traced here: 74.8 us
  Pallas kernels  74.2 us (99%)
    pallas_call x1, Pallas kernels, on_device(): pl.pallas_call(kernel, out_shape=[v(o.shape, o.dtype) for o in out], in_s...  73 us

profile of v5, /device:TPU:32, one launch (start us, length us, event | category | flops | bytes accessed | tf_op | source)
XLA Modules:
  0.0 74.8 jit_solution(15156265808727425786)
XLA Ops:
  0.6 73.0 %shard_map.119 = (f32[32,2048]{1,0:T(8,128)S(1)}, f32[32,2048]{1,0:T(8,128)S(1)}, bf16[32,8192]{1,0:T(8,128)(2,1)S(1)}, bf16[1,320,512]{2,1,0:T(8,128)(2,1)S(1)}, f32[1,128,512]{2,1,0:T(8,128)S(1)}) custom-call(bf16[1,32,8192]{2,1,0:T(8,128)(2,1)} %lp.1, bf16[32,8192]{1,0:T(8,128)(2,1)} %an.1, f32[1,32,8192]{2,1,0:T(8,128)} %fb.1, f32[32,2048]{1,0:T(8,128)} %ms.1, ...), custom_call_target="tpu_custom_call" | custom-call | flops 5368709120 | bytes 12582912 | tf_op jit(solution)/shard_map/pallas_call | solution.py:476
  73.6 1.2 %shard_map.120 = (f32[32,2048]{1,0:T(8,128)}, f32[32,2048]{1,0:T(8,128)}, bf16[32,8192]{1,0:T(8,128)(2,1)}, bf16[1,320,512]{2,1,0:T(8,128)(2,1)}, f32[1,128,512]{2,1,0:T(8,128)}) custom-call(f32[32,2048]{1,0:T(8,128)S(1)} %get-tuple-element.10.refs_0_, f32[32,2048]{1,0:T(8,128)S(1)} %get-tuple-element.11.refs_1_, ...), custom_call_target="tpu_custom_call" | custom-call | tf_op jit(solution)/shard_map/pallas_call | solution.py:490

commit v6 on v5

--- a/solution.py
+++ b/solution.py
@@ -419,10 +419,10 @@
     both(mid3, 1)
     both(mid3, -1)
     both(keys, 0)
+    both(end1, 0)
+    both(end3)
     outer_end()
     drain()
-    both(end1, 0)
-    both(end3)
     keys_end()
     drain()
 

time: 74.9 us -> 75.2 us (level)
  no operation moved by 1% of the time
where the time goes in v6:
time: 75.2 us; the launch traced here: 75.1 us
  Pallas kernels  74.5 us (99%)
    pallas_call x1, Pallas kernels, on_device(): pl.pallas_call(kernel, out_shape=[v(o.shape, o.dtype) for o in out], in_s...  73.3 us

profile of v6, /device:TPU:32, one launch (start us, length us, event | category | flops | bytes accessed | tf_op | source)
XLA Modules:
  0.0 75.1 jit_solution(1724758828294168871)
XLA Ops:
  0.6 73.3 %shard_map.119 = (f32[32,2048]{1,0:T(8,128)S(1)}, f32[32,2048]{1,0:T(8,128)S(1)}, bf16[32,8192]{1,0:T(8,128)(2,1)S(1)}, bf16[1,320,512]{2,1,0:T(8,128)(2,1)S(1)}, f32[1,128,512]{2,1,0:T(8,128)S(1)}) custom-call(bf16[1,32,8192]{2,1,0:T(8,128)(2,1)} %lp.1, bf16[32,8192]{1,0:T(8,128)(2,1)} %an.1, f32[1,32,8192]{2,1,0:T(8,128)} %fb.1, f32[32,2048]{1,0:T(8,128)} %ms.1, ...), custom_call_target="tpu_custom_call" | custom-call | flops 5368709120 | bytes 12582912 | tf_op jit(solution)/shard_map/pallas_call | solution.py:476
  73.9 1.2 %shard_map.120 = (f32[32,2048]{1,0:T(8,128)}, f32[32,2048]{1,0:T(8,128)}, bf16[32,8192]{1,0:T(8,128)(2,1)}, bf16[1,320,512]{2,1,0:T(8,128)(2,1)}, f32[1,128,512]{2,1,0:T(8,128)}) custom-call(f32[32,2048]{1,0:T(8,128)S(1)} %get-tuple-element.10.refs_0_, f32[32,2048]{1,0:T(8,128)S(1)} %get-tuple-element.11.refs_1_, ...), custom_call_target="tpu_custom_call" | custom-call | tf_op jit(solution)/shard_map/pallas_call | solution.py:490
